TPU v7x, 32 devices: a whole 2x2x4 slice. The times are simulated.
32 devices in a mesh: ctx: 8 (over z, core), dp: 4 (over y, x).
Axes of the slice: x: 2, y: 2, z: 4, core: 2. Of those that a mesh axis runs over, the one named last changes fastest.
Arguments:
- stream: bfloat16 [3, 1024, 8192], P(None, 'ctx', 'dp'), may hold values from -6 to 6
- short_taps: float32 [3, 3, 8192], replicated, may hold values from -3.5 to 3.5
- decay_rate: float32 [16, 512], P('dp'), may hold values from 0.0001953125 to 0.1
- residue: float32 [16, 512], P('dp'), may hold values from -0.4472136 to 0.4472136
Outputs:
- gated_output: bfloat16 [1024, 8192], P('ctx', 'dp')
All inputs are finite; a program needn't handle non-finite values.
Results may differ from a plain program's by a relative error of at most 0.002.
Values may be sent and summed in bfloat16 or wider, within the bound.
A program may use at most 128 MiB of HBM per device.

v0:
```python
import math

import jax
import jax.numpy as jnp
from jax import lax
from jax.sharding import PartitionSpec as P

GROUP = 16
ORDER = 16


def from_behind(block, axis, distance):
    devices = range(lax.axis_size(axis))
    route = [(i - distance, i) for i in devices if i - distance in devices]
    return lax.ppermute(block, axis, route)


def unfold_taps(seq_taps):
    group_count, length = seq_taps.shape
    padded = jnp.concatenate([seq_taps, jnp.zeros((group_count, length + 1), seq_taps.dtype)], 1)
    tiled = jnp.tile(padded, (1, length))[:, : 2 * length * length]
    return tiled.reshape(group_count, length, 2 * length)[:, :, :length]


def shards(stream, short_taps, decay_rate, residue):
    row_count = stream.shape[1]
    chan_count = stream.shape[2]
    local_groups = chan_count // GROUP
    reach = short_taps.shape[1] - 1
    earlier_rows = from_behind(stream[:, row_count - reach :, :], "ctx", 1)
    extended = jnp.concatenate([earlier_rows, stream], 1)
    dp_index = lax.axis_index("dp")
    local_taps = lax.dynamic_slice_in_dim(short_taps, dp_index * chan_count, chan_count, 2)
    features = local_taps[:, 0, None, :] * extended[:, reach:, :].astype(jnp.float32)
    for lag in range(1, reach + 1):
        features = features + local_taps[:, lag, None, :] * extended[
            :, reach - lag : reach - lag + row_count, :
        ].astype(jnp.float32)
    query = features[0]
    product = features[1] * features[2]
    rate_local, residue_local = (
        lax.all_to_all(decay_rate, "dp", split_axis=1, concat_axis=0, tiled=True),
        lax.all_to_all(residue, "dp", split_axis=1, concat_axis=0, tiled=True),
    )
    block = math.gcd(row_count, 128)
    sub_count = row_count // block
    inner_pos = jnp.arange(block, dtype=jnp.float32)
    powers = jnp.exp(-rate_local[:, :, None] * inner_pos)
    seq_taps = jnp.sum(residue_local[:, :, None] * powers, 0)
    toeplitz = unfold_taps(seq_taps)
    close_inner = jnp.exp(-rate_local[:, :, None] * (block - 1.0 - inner_pos))
    open_inner = residue_local[:, :, None] * jnp.exp(-rate_local[:, :, None] * (inner_pos + 1.0))
    span_inner = jnp.exp(-rate_local * block)
    sub_blocks = product.reshape(sub_count, block, local_groups, GROUP)

    def advance(state, piece):
        inside = jnp.einsum("gst,sgc->tgc", toeplitz, piece, precision=lax.Precision.HIGHEST)
        carried = jnp.einsum("rgt,rgc->tgc", open_inner, state, precision=lax.Precision.HIGHEST)
        fresh = jnp.einsum("rgs,sgc->rgc", close_inner, piece, precision=lax.Precision.HIGHEST)
        return (span_inner[:, :, None] * state + fresh, inside + carried)

    start_state = jnp.zeros((ORDER, local_groups, GROUP), jnp.float32)
    unused_state, local_part = lax.scan(advance, start_state, sub_blocks)
    local_part = local_part.reshape(row_count, local_groups, GROUP)
    grouped = product.reshape(row_count, local_groups, GROUP)
    position = jnp.arange(row_count, dtype=jnp.float32)
    closing = jnp.exp(-rate_local[:, :, None] * (row_count - 1.0 - position))
    end_state = jnp.einsum(
        "rgs,sgc->rgc", closing, grouped, precision=lax.Precision.HIGHEST
    ).reshape(ORDER, chan_count)
    ctx_index = lax.axis_index("ctx")
    piece = lax.all_gather(end_state[None], "ctx", axis=0, tiled=True)
    count = piece.shape[0]
    distance = (ctx_index - 1 - jnp.arange(count, dtype=jnp.int32)).astype(jnp.float32)
    live_mask = (distance >= 0.0).astype(jnp.float32)
    weight = (
        jnp.exp(-rate_local[None] * row_count * jnp.maximum(distance, 0.0)[:, None, None])
        * live_mask[:, None, None]
    )
    summed = jnp.einsum(
        "krg,krgc->rgc",
        weight,
        piece.reshape(count, ORDER, local_groups, GROUP),
        precision=lax.Precision.HIGHEST,
    )
    incoming = summed.reshape(ORDER, chan_count)
    opening = residue_local[:, :, None] * jnp.exp(-rate_local[:, :, None] * (position + 1.0))
    tail_part = jnp.einsum(
        "rgt,rgc->tgc",
        opening,
        incoming.reshape(ORDER, local_groups, GROUP),
        precision=lax.Precision.HIGHEST,
    )
    convolved = (local_part + tail_part).reshape(row_count, chan_count)
    return (query * convolved).astype(jnp.bfloat16)


def solution(mesh):
    in_specs = (P(None, "ctx", "dp"), P(), P("dp", None), P("dp", None))
    out_specs = P("ctx", "dp")
    return jax.shard_map(shards, mesh=mesh, in_specs=in_specs, out_specs=out_specs, check_vma=False)
```

profile of v0, /device:TPU:0, one launch (start us, length us, event | category | flops | bytes accessed | tf_op | source)
XLA Modules:
  0.0 124.4 jit_solution(14423307194204922870)
XLA Ops:
  6.5 0.9 slice.35
  7.5 2.4 %collective-permute-start = (bf16[3,2,2048]{2,1,0:T(2,128)(2,1)S(1)}, bf16[3,2,2048]{2,1,0:T(2,128)(2,1)S(1)}, u32[]{:S(2)}, u32[]{:S(2)}) collective-permute-start(bf16[3,2,2048]{2,1,0:T(2,128)(2,1)S(1)} %slice.35), channel_id=1, source_target_pairs={{0,4},{4,8},{8,12},{12,16},{16,20},{20,24},{24,28},{1,5},{5,9},{9,... | collective-permute-start | bytes 73736 | tf_op jit(solution)/shard_map/ppermute | solution.py:15
  9.8 4.6 %all-to-all-start.1 = ((f32[4,4,128]{2,0,1:T(4,128)}), f32[4,4,128]{2,0,1:T(4,128)S(1)}, u32[]{:S(2)}, u32[]{:S(2)}) async-start(f32[4,4,128]{2,0,1:T(4,128)} %bitcast.47), calls=%async_computation.1 | async-start | bytes 16384 | tf_op jit(solution)/shard_map/all_to_all | solution.py:42
  14.4 0.0 all-gather.2.cloned.1.call-start
  14.4 1.2 constant_dynamic-slice_fusion.1
  15.6 2.6 %copy.29 = bf16[3,128,2048]{1,2,0:T(8,128)(2,1)} copy(bf16[3,128,2048]{2,1,0:T(8,128)(2,1)} %param.4) | data formatting | bytes 3145728 | tf_op args[0]
  18.3 0.8 all-to-all-done.1
  19.1 0.1 copy.35
  19.2 0.0 collective-permute-done
  19.2 1.6 %copy.30 = bf16[3,2,2048]{1,2,0:T(8,128)(2,1)} copy(bf16[3,2,2048]{2,1,0:T(2,128)(2,1)S(1)} %collective-permute-done) | data formatting | bytes 49152 | tf_op jit(solution)/shard_map/ppermute | solution.py:15
  20.8 8.2 %multiply_add_fusion = f32[3,128,2048]{1,2,0:T(8,128)S(1)} fusion(bf16[3,128,2048]{1,2,0:T(8,128)(2,1)} %copy.29, bf16[3,2,2048]{1,2,0:T(8,128)(2,1)} %copy.30, f32[3,2048]{1,0:T(4,128)S(1)} %get-tuple-element.22, f32[3,2048]{1,0:T(4,128)S(1)} %get-tuple-element.23, f32[3,2048]{1,0:T(4,128)S(1)} %bitcast.43), kind=kLoop, calls=%fused_computation.3 | loop fusion | flops 11010048 | bytes 4816896 | tf_op jit(solution)/shard_map/add | solution.py:36
  29.0 0.1 slice_multiply_fusion
  29.1 0.0 copy-start
  29.1 1.0 copy-done
  30.1 2.8 %fusion.4 = f32[128,16,16]{2,1,0:T(8,128)} fusion(f32[128,128,16]{0,2,1:T(8,128)S(1)} %bitcast.40, f32[128]{0:T(128)S(1)} %iota_subtract_fusion, f32[16,128]{0,1:T(8,128)S(1)} %copy.35), kind=kOutput, calls=%fused_computation.13 | convolution fusion | flops 50593792 | bytes 1188352 | tf_op jit(solution)/shard_map/rgs,sgc->rgc/dot_general | solution.py:68
  32.9 2.2 %copy.38 = f32[1,16,2048]{2,1,0:T(8,128)} copy(f32[1,16,2048]{1,2,0:T(8,128)} %bitcast.42) | data formatting | bytes 262144 | tf_op jit(solution)/shard_map/broadcast_in_dim;reshape | solution.py:72
  35.1 0.0 all-gather.2.cloned.1.call-update
  35.1 3.4 %all-to-all-start = ((f32[4,4,128]{2,0,1:T(4,128)}), f32[4,4,128]{2,0,1:T(4,128)S(1)}, u32[]{:S(2)}, u32[]{:S(2)}) async-start(f32[4,4,128]{2,0,1:T(4,128)} %bitcast.4), calls=%async_computation | async-start | bytes 16384 | tf_op jit(solution)/shard_map/all_to_all | solution.py:43
  38.6 4.6 %all-to-all-done = f32[4,4,128]{2,0,1:T(4,128)S(1)} async-done(((f32[4,4,128]{2,0,1:T(4,128)}), f32[4,4,128]{2,0,1:T(4,128)S(1)}, u32[]{:S(2)}, u32[]{:S(2)}) %all-to-all-start) | async-done | bytes 8224 | tf_op jit(solution)/shard_map/all_to_all | solution.py:43
  43.3 0.1 copy.33
  43.4 0.6 multiply_reduce_fusion.1
  44.0 0.1 copy.54
  44.1 7.0 %tile.4 = f32[128,128,257]{0,2,1:T(8,128)} broadcast(f32[128,257]{0,1:T(8,128)S(1)} %concatenate.7.clone), dimensions={0,2} | broadcast | bytes 16974336 | tf_op jit(solution)/shard_map/tile | solution.py:21
  51.1 17.6 %tile.10 = f32[128,32896]{0,1:T(8,128)} reshape(f32[128,128,257]{0,2,1:T(8,128)} %tile.4) | data formatting | bytes 33685504 | tf_op jit(solution)/shard_map/tile | solution.py:21
  68.7 0.0 slice-start
  68.7 5.8 %slice-done = f32[128,32768]{0,1:T(8,128)S(1)} async-done(((f32[128,32896]{0,1:T(8,128)}), f32[128,32768]{0,1:T(8,128)S(1)}, s32[]{:S(2)}) %slice-start) | async-done | bytes 16777240 | tf_op jit(solution)/shard_map/slice | solution.py:21
  74.5 3.8 %slice.50 = f32[128,128,128]{0,2,1:T(8,128)} slice(f32[128,128,256]{0,2,1:T(8,128)S(1)} %bitcast.39), slice={[0:128], [0:128], [0:128]} | slice | bytes 16777216 | tf_op jit(solution)/shard_map/slice | solution.py:22
  78.3 9.3 %copy.52 = f32[128,128,128]{2,1,0:T(8,128)} copy(f32[128,128,128]{0,2,1:T(8,128)} %slice.50) | data formatting | bytes 16777216
  87.6 0.1 multiply_bitcast_fusion
  87.7 9.7 %fusion.17 = f32[128,16,128]{2,1,0:T(8,128)S(1)} fusion(f32[128,128,16]{0,2,1:T(8,128)} %bitcast.41, f32[128,128,128]{2,1,0:T(8,128)} %copy.52), kind=kOutput, calls=%fused_computation.41 | convolution fusion | flops 402653184 | bytes 10485760 | tf_op jit(solution)/shard_map/while/body/eval_jaxpr/gst,sgc->tgc/dot_general | solution.py:57
  97.4 2.5 %convolution_add_fusion.1 = f32[128,16,128]{2,1,0:T(8,128)} fusion(f32[128,16,128]{2,1,0:T(8,128)S(1)} %fusion.17, f32[128]{0:T(128)S(1)} %iota_add_fusion, f32[16,128]{0,1:T(8,128)S(1)} %copy.35, f32[16,128]{0,1:T(8,128)S(1)} %copy.33), kind=kOutput, calls=%fused_computation.7 | convolution fusion | flops 51118080 | bytes 2114048 | tf_op jit(solution)/shard_map/while/body/eval_jaxpr/rgt,rgc->tgc/dot_general | solution.py:58
  99.9 0.0 all-gather.2.cloned.1.call-done
  99.9 6.2 %reshape.69 = f32[8,16,128,16]{3,2,1,0:T(8,128)} reshape(f32[8,16,2048]{2,1,0:T(8,128)} %all-gather.2.cloned.1.call-done) | data formatting | bytes 2097152 | tf_op jit(solution)/shard_map/reshape | solution.py:83
  106.0 0.0 copy-start.1
  106.1 5.6 %multiply_reduce_fusion = f32[16,128,16]{2,1,0:T(8,128)S(1)} fusion(f32[8,16,128,16]{3,2,1,0:T(8,128)} %reshape.69, f32[16,128,8]{1,0,2:T(8,128)S(1)} %multiply_bitcast_fusion), kind=kLoop, calls=%fused_computation | loop fusion | flops 491520 | bytes 1245184
  111.6 0.0 copy-done.1
  111.7 2.9 %convolution_add_fusion = f32[128,16,128]{2,1,0:T(8,128)S(1)} fusion(f32[128,16,128]{2,1,0:T(8,128)S(1)} %copy-done.1, f32[16,128,16]{2,1,0:T(8,128)S(1)} %multiply_reduce_fusion, f32[128]{0:T(128)S(1)} %iota_add_fusion, f32[16,128]{0,1:T(8,128)S(1)} %copy.35, f32[16,128]{0,1:T(8,128)S(1)} %copy.33), kind=kOutput, calls=%fused_computation.6 | convolution fusion | flops 51118080 | bytes 2245120 | tf_op jit(solution)/shard_map/rgt,rgc->tgc/dot_general | solution.py:88
  114.6 0.9 fusion.2
  115.5 2.0 %copy.39 = bf16[128,2048]{1,0:T(8,128)(2,1)} copy(bf16[128,2048]{0,1:T(8,128)(2,1)} %fusion.2) | data formatting | bytes 1048576 | tf_op jit(solution)/shard_map/convert_element_type | solution.py:95
  (9 shorter events, 0.1 us)
Async XLA Ops:
  7.5 11.7 %collective-permute-start = (bf16[3,2,2048]{2,1,0:T(2,128)(2,1)S(1)}, bf16[3,2,2048]{2,1,0:T(2,128)(2,1)S(1)}, u32[]{:S(2)}, u32[]{:S(2)}) collective-permute-start(bf16[3,2,2048]{2,1,0:T(2,128)(2,1)S(1)} %slice.35), channel_id=1, source_target_pairs={{0,4},{4,8},{8,12},{12,16},{16,20},{20,24},{24,28},{1,5},{5,9},{9,... | collective-permute-start | bytes 73736 | tf_op jit(solution)/shard_map/ppermute | solution.py:15
  9.8 9.2 %all-to-all-start.1 = ((f32[4,4,128]{2,0,1:T(4,128)}), f32[4,4,128]{2,0,1:T(4,128)S(1)}, u32[]{:S(2)}, u32[]{:S(2)}) async-start(f32[4,4,128]{2,0,1:T(4,128)} %bitcast.47), calls=%async_computation.1 | async-start | bytes 16384 | tf_op jit(solution)/shard_map/all_to_all | solution.py:42
  14.4 85.5 %all-gather.2.cloned.1.call-start = ((), (), s32[]{:S(2)}) async-start(), calls=%async_computation.2 | async-start | bytes 1179648 | tf_op jit(solution)/shard_map/all_gather | solution.py:72
  29.1 1.0 copy-start
  35.1 8.1 %all-to-all-start = ((f32[4,4,128]{2,0,1:T(4,128)}), f32[4,4,128]{2,0,1:T(4,128)S(1)}, u32[]{:S(2)}, u32[]{:S(2)}) async-start(f32[4,4,128]{2,0,1:T(4,128)} %bitcast.4), calls=%async_computation | async-start | bytes 16384 | tf_op jit(solution)/shard_map/all_to_all | solution.py:43
  68.7 5.8 %slice-start = ((f32[128,32896]{0,1:T(8,128)}), f32[128,32768]{0,1:T(8,128)S(1)}, s32[]{:S(2)}) async-start(f32[128,32896]{0,1:T(8,128)} %tile.10), calls=%async_computation.3 | async-start | bytes 33554432 | tf_op jit(solution)/shard_map/slice | solution.py:21
  106.0 5.6 %copy-start.1 = (f32[128,16,128]{2,1,0:T(8,128)S(1)}, f32[128,16,128]{2,1,0:T(8,128)}, u32[]{:S(2)}) copy-start(f32[128,16,128]{2,1,0:T(8,128)} %convolution_add_fusion.1) | copy-start | bytes 3145732
Sparse Core Ops, SparseCore 0:
  35.3 23.1 all-gather.1
where the time goes:
time: 126 us; the launch traced here: 124 us
  local copies, waits for them, and re-layouts  61.6 us (49%)
  matrix products  17.9 us (14%)
  other arithmetic  15.6 us (12%)
  between operations  13.5 us (11%)
  starting transfers between devices  10.4 us (8%)
  waiting for transfers between devices  5.46 us (4%)
    another operation x2, local copies, waits for them, and re-layouts, unfold_taps(): tiled = jnp.tile(padded, (1, length))[:, :2 * length * length]  24.6 us
    unnamed x9, local copies, waits for them, and re-layouts  13 us
    dot_general x1, matrix products, advance(): jnp.einsum('gst,sgc->tgc', toeplitz, piece, precision=lax.Precision.HIGHEST)  9.66 us
    add x1, other arithmetic, shards(): features + local_taps[:, lag, None, :] * extended[:, reach - lag:reach -...  8.21 us
    reshape x1, local copies, waits for them, and re-layouts, shards(): piece.reshape(count, ORDER, local_groups, GROUP)  6.19 us
    slice x2, local copies, waits for them, and re-layouts, unfold_taps(): tiled = jnp.tile(padded, (1, length))[:, :2 * length * length]  5.77 us
    unnamed x2, other arithmetic  5.67 us
    all_to_all x1, waiting for transfers between devices, shards(): lax.all_to_all(residue, 'dp', split_axis=1, concat_axis=0, tiled=True)  4.61 us
  transfers between devices with their start and end apart: 4, of which 2 were waited for; matrix products, arithmetic and copies ran while one was open for 44% of the time, Pallas kernels for 0%

commit v1 on v0

v1 whole, which is shorter than its diff:
```python
import functools

import jax
import jax.numpy as jnp
from jax import lax
from jax.experimental import pallas as pl
from jax.experimental.pallas import tpu as pltpu
from jax.sharding import PartitionSpec as P

GROUP = 16
LANES = 128
CHUNKS = 2
DICT = pl.DeviceIdType.MESH


def kernel(
    n_ctx, n_dp,
    stream, taps, rate, resid, out,
    xv, tp, rates, resids, hs, hr, x0, prod, query, conv, sel, dec, amp, span, end, end_in,
    chain_in, other_in, chain_out, zs,
    local_sem, dp_send, dp_recv, halo_sem, end_send, end_recv, chain_send, chain_recv, fwd_send, fwd_recv,
):
    k = lax.axis_index("ctx")
    dp = lax.axis_index("dp")
    core = lax.rem(k, 2)
    z = k // 2
    last_z = n_ctx // 2 - 1
    partner = k + 1 - 2 * core
    T, C = stream.shape[1], stream.shape[2]
    J = C // LANES
    HJ = J // 2
    reach = taps.shape[1] - 1
    own_poles, G = rate.shape
    R = own_poles * n_dp
    RC = R // CHUNKS
    blocks = T // 16
    f32 = jnp.float32

    loads = []
    for n, i in enumerate((1, 2, 0)):
        loads.append(pltpu.make_async_copy(stream.at[i], xv.at[i], local_sem.at[n]))
    loads.append(pltpu.make_async_copy(taps.at[:, :, pl.ds(pl.multiple_of(dp * C, LANES), C)], tp, local_sem.at[3]))
    own_rate = pltpu.make_async_copy(rate, rates.at[dp], local_sem.at[4])
    own_resid = pltpu.make_async_copy(resid, resids.at[dp], local_sem.at[5])
    for c in loads:
        c.start()
    own_rate.start()
    own_resid.start()

    barrier = pltpu.get_barrier_semaphore()

    def greet(**where):
        pl.semaphore_signal(barrier, inc=1, device_id=where, device_id_type=DICT)

    for d in range(1, n_dp):
        greet(dp=lax.rem(dp + d, n_dp))
    greet(ctx=partner)
    beside = k - 1 + 2 * core
    has_beside = jnp.logical_and(beside >= 0, beside < n_ctx)
    has_prev, has_next = z > 0, z < last_z

    @pl.when(has_beside)
    def _():
        greet(ctx=beside)

    @pl.when(has_prev)
    def _():
        greet(ctx=k - 2)

    @pl.when(has_next)
    def _():
        greet(ctx=k + 2)

    pl.semaphore_wait(
        barrier,
        n_dp + has_beside.astype(jnp.int32) + has_prev.astype(jnp.int32) + has_next.astype(jnp.int32),
    )

    def dp_copy(which, d, owner, peer):
        src, dst = ((rate, rates), (resid, resids))[which]
        return pltpu.make_async_remote_copy(
            src_ref=src, dst_ref=dst.at[owner], send_sem=dp_send.at[which, d - 1],
            recv_sem=dp_recv.at[which, d - 1], device_id={"dp": peer}, device_id_type=DICT)

    for d in range(1, n_dp):
        for which in range(2):
            dp_copy(which, d, dp, lax.rem(dp + d, n_dp)).start()

    for c in loads:
        c.wait()
    for i in range(3):
        hs[i] = xv[i, T - 16:T, :].astype(f32)[16 - reach:16]

    def halo():
        return pltpu.make_async_remote_copy(
            src_ref=hs, dst_ref=hr, send_sem=halo_sem.at[0], recv_sem=halo_sem.at[1],
            device_id={"ctx": k + 1}, device_id_type=DICT)

    @pl.when(k < n_ctx - 1)
    def _():
        halo().start()

    def feature(i, j, window):
        cols = pl.ds(j * LANES, LANES)
        total = tp[i, 0:1, cols] * window[8:24]
        for lag in range(1, reach + 1):
            total = total + tp[i, lag:lag + 1, cols] * window[8 - lag:24 - lag]
        return total

    def window_at(i, j, b):
        cols = pl.ds(j * LANES, LANES)
        before = xv[i, pl.ds(pl.multiple_of(b * 16 - 16, 16), 16), cols].astype(f32)
        here = xv[i, pl.ds(pl.multiple_of(b * 16, 16), 16), cols].astype(f32)
        return jnp.concatenate([before[8:16], here], 0)

    def window_first(i, j):
        return x0[i, :, pl.ds(j * LANES, LANES)]

    def put(ref, b, j, tile):
        for u in range(2):
            ref[pl.ds(pl.multiple_of(((2 * b + u) * J + j) * 8, 8), 8), :] = tile[8 * u:8 * u + 8]

    @pl.loop(1, blocks)
    def _(b):
        for j in range(J):
            put(prod, b, j, feature(1, j, window_at(1, j, b)) * feature(2, j, window_at(2, j, b)))

    own_rate.wait()
    own_resid.wait()
    for d in range(1, n_dp):
        for which in range(2):
            dp_copy(which, d, lax.rem(dp + n_dp - d, n_dp), dp).wait_recv()

    per_tile = LANES // GROUP
    tile_of = lax.broadcasted_iota(jnp.int32, (HJ, G), 1) // per_tile
    row = lax.broadcasted_iota(jnp.int32, (HJ, G), 0)
    spread = (
        lax.rem(lax.broadcasted_iota(jnp.int32, (G, LANES), 0), per_tile)
        == lax.broadcasted_iota(jnp.int32, (G, LANES), 1) // GROUP
    ).astype(f32)
    for source, is_rate in ((rates, True), (resids, False)):
        for h in range(2):
            mask = tile_of == dp * J + h * HJ + row
            for r in range(R):
                line = source[r // own_poles, r % own_poles:r % own_poles + 1, :]
                sel[(h * R + r) * HJ:(h * R + r + 1) * HJ, :] = jnp.where(mask, line, 0.0)
        wide = jnp.dot(sel[...], spread, precision=lax.Precision.HIGHEST, preferred_element_type=f32)
        for h in range(2):
            for r in range(R):
                part = wide[(h * R + r) * HJ:(h * R + r + 1) * HJ]
                if is_rate:
                    dec[h, r] = jnp.exp(-part)
                    span[h, r] = jnp.exp(-part * T)
                else:
                    amp[h, r] = part

    @pl.when(k == 0)
    def _():
        hr[...] = jnp.zeros_like(hr)

    @pl.when(k > 0)
    def _():
        halo().wait_recv()

    for i in range(3):
        x0[i, 8 - reach:8, :] = hr[i]
        x0[i, 8:24, :] = xv[i, 0:16, :].astype(f32)
    for j in range(J):
        put(prod, 0, j, feature(1, j, window_first(1, j)) * feature(2, j, window_first(2, j)))

    def rows(tb, h, u):
        return pl.ds(tb * (J * 8) + h * (HJ * 8) + u, HJ, stride=8)

    def close(h):
        decay = [dec[h, r] for r in range(R)]

        def body(tb, state):
            for u in range(8):
                x = prod[rows(tb, h, u), :]
                state = tuple(a * s + x for a, s in zip(decay, state))
            return state

        state = lax.fori_loop(0, T // 8, body, tuple(jnp.zeros((HJ, LANES), f32) for _ in range(R)))
        for r in range(R):
            end[h, r] = state[r]

    def end_copy(h):
        return pltpu.make_async_remote_copy(
            src_ref=end.at[h], dst_ref=end_in.at[h], send_sem=end_send.at[h], recv_sem=end_recv.at[h],
            device_id={"ctx": partner}, device_id_type=DICT)

    close(1 - core)
    end_copy(1 - core).start()
    close(core)

    @pl.when(core == 0)
    def _():
        end_copy(0).start()

    def total_of_chip():
        end_copy(core).wait_recv()
        for r in range(R):
            own, other = end[core, r], end_in[core, r]
            first = jnp.where(core == 0, own, other)
            second = jnp.where(core == 0, other, own)
            chain_out[r // RC, r % RC] = span[core, r] * first + second

    def chain_copy(c):
        return pltpu.make_async_remote_copy(
            src_ref=chain_out.at[c], dst_ref=chain_in.at[c], send_sem=chain_send.at[c],
            recv_sem=chain_recv.at[c], device_id={"ctx": k + 2}, device_id_type=DICT)

    def forward(c):
        return pltpu.make_async_remote_copy(
            src_ref=chain_in.at[c], dst_ref=other_in.at[c], send_sem=fwd_send.at[c],
            recv_sem=fwd_recv.at[c], device_id={"ctx": partner}, device_id_type=DICT)

    def relay():
        for c in range(CHUNKS):
            chain_copy(c).wait_recv()

            @pl.when(has_next)
            def _():
                for q in range(RC):
                    leap = span[core, c * RC + q]
                    chain_out[c, q] = chain_out[c, q] + leap * leap * chain_in[c, q]
                chain_copy(c).start()

            forward(c).start()

    total_of_chip()

    @pl.when(z == 0)
    def _():
        for c in range(CHUNKS):
            @pl.when(has_next)
            def _():
                chain_copy(c).start()
        chain_in[...] = jnp.zeros_like(chain_in)
        other_in[...] = jnp.zeros_like(other_in)

    for j in range(J):
        put(query, 0, j, feature(0, j, window_first(0, j)))

    @pl.loop(1, blocks)
    def _(b):
        for j in range(J):
            put(query, b, j, feature(0, j, window_at(0, j, b)))

    def inside(h):
        decay = [dec[h, r] for r in range(R)]
        gain = [amp[h, r] for r in range(R)]

        def body(tb, state):
            for u in range(8):
                x = prod[rows(tb, h, u), :]
                state = tuple(a * s + x for a, s in zip(decay, state))
                terms = [g * s for g, s in zip(gain, state)]
                while len(terms) > 1:
                    terms = [sum(terms[n:n + 2][1:], terms[n]) for n in range(0, len(terms), 2)]
                conv[rows(tb, h, u), :] = terms[0]
            return state

        lax.fori_loop(0, T // 8, body, tuple(jnp.zeros((HJ, LANES), f32) for _ in range(R)))

    inside(0)

    @pl.when(z == 1)
    def _():
        relay()

    inside(1)

    @pl.when(z > 1)
    def _():
        relay()

    @pl.when(core == 1)
    def _():
        end_copy(0).wait_recv()

    def tail(h, source):
        for r in range(R):
            zs[r] = source[r // RC, r % RC]

        @pl.when(core == 1)
        def _():
            for r in range(R):
                zs[r] = span[h, r] * zs[r] + end_in[h, r]

        decay = [dec[h, r] for r in range(R)]

        def body(tb, state):
            for u in range(8):
                state = tuple(a * s for a, s in zip(decay, state))
                terms = list(state)
                while len(terms) > 1:
                    terms = [sum(terms[n:n + 2][1:], terms[n]) for n in range(0, len(terms), 2)]
                conv[rows(tb, h, u), :] = conv[rows(tb, h, u), :] + terms[0]
            return state

        lax.fori_loop(0, T // 8, body, tuple(amp[h, r] * zs[r] for r in range(R)))

    tail(core, chain_in)

    @pl.when(has_prev)
    def _():
        for c in range(CHUNKS):
            forward(c).wait_recv()

    tail(1 - core, other_in)

    @pl.loop(0, blocks)
    def _(b):
        for j in range(J):
            tiles = []
            for u in range(2):
                at = pl.ds(pl.multiple_of(((2 * b + u) * J + j) * 8, 8), 8)
                tiles.append(query[at, :] * conv[at, :])
            out[pl.ds(pl.multiple_of(b * 16, 16), 16), pl.ds(j * LANES, LANES)] = jnp.concatenate(
                tiles, 0).astype(out.dtype)

    for d in range(1, n_dp):
        for which in range(2):
            dp_copy(which, d, dp, lax.rem(dp + d, n_dp)).wait_send()

    @pl.when(k < n_ctx - 1)
    def _():
        halo().wait_send()

    end_copy(1 - core).wait_send()

    @pl.when(core == 0)
    def _():
        end_copy(0).wait_send()

    for c in range(CHUNKS):
        @pl.when(has_next)
        def _():
            chain_copy(c).wait_send()

        @pl.when(has_prev)
        def _():
            forward(c).wait_send()


def solution(mesh):
    n_ctx, n_dp = mesh.shape["ctx"], mesh.shape["dp"]

    def shards(stream, short_taps, decay_rate, residue):
        T, C = stream.shape[1], stream.shape[2]
        n_taps = short_taps.shape[1]
        own_poles, G = decay_rate.shape
        R = own_poles * n_dp
        HJ = C // LANES // 2
        RC = R // CHUNKS
        f32 = jnp.float32
        dma = pltpu.SemaphoreType.DMA
        flat = pltpu.VMEM((T * C // LANES, LANES), f32)
        halves = pltpu.VMEM((2, R, HJ, LANES), f32)
        piece = pltpu.VMEM((CHUNKS, RC, HJ, LANES), f32)
        edge = pltpu.VMEM((3, n_taps - 1, C), f32)
        return pl.pallas_call(
            functools.partial(kernel, n_ctx, n_dp),
            out_shape=jax.ShapeDtypeStruct((T, C), jnp.bfloat16),
            in_specs=[pl.BlockSpec(memory_space=pl.ANY)] * 4,
            out_specs=pl.BlockSpec(memory_space=pltpu.VMEM),
            scratch_shapes=[
                pltpu.VMEM((3, T, C), jnp.bfloat16),
                pltpu.VMEM((3, n_taps, C), f32),
                pltpu.VMEM((n_dp, own_poles, G), f32),
                pltpu.VMEM((n_dp, own_poles, G), f32),
                edge, edge,
                pltpu.VMEM((3, 24, C), f32),
                flat, flat, flat,
                pltpu.VMEM((2 * R * HJ, G), f32),
                halves, halves, halves, halves, halves,
                piece, piece, piece,
                pltpu.VMEM((R, HJ, LANES), f32),
                dma((6,)),
                dma((2, n_dp - 1)), dma((2, n_dp - 1)),
                dma((2,)),
                dma((2,)), dma((2,)),
                dma((CHUNKS,)), dma((CHUNKS,)),
                dma((CHUNKS,)), dma((CHUNKS,)),
            ],
            compiler_params=pltpu.CompilerParams(
                collective_id=0, has_side_effects=True, vmem_limit_bytes=32 * 1024 * 1024),
            cost_estimate=pl.CostEstimate(
                flops=8 * R * T * C, bytes_accessed=8 * T * C, transcendentals=0),
        )(stream, short_taps, decay_rate, residue)

    in_specs = (P(None, "ctx", "dp"), P(), P("dp", None), P("dp", None))
    return jax.shard_map(shards, mesh=mesh, in_specs=in_specs, out_specs=P("ctx", "dp"), check_vma=False)
```

time: 126 us -> 23.9 us (0.19)
  the two profiles are of different devices: /device:TPU:0 before, /device:TPU:25 now
where the time goes in v1:
time: 23.9 us; the launch traced here: 23.6 us
  Pallas kernels  19 us (79%)
  local copies, waits for them, and re-layouts  4.59 us (19%)
    pallas_call x1, Pallas kernels, shards(): pl.pallas_call(functools.partial(kernel, n_ctx, n_dp), out_shape=jax.Shap...  19 us
    unnamed x9, local copies, waits for them, and re-layouts  4.59 us

profile of v1, /device:TPU:25, one launch (start us, length us, event | category | flops | bytes accessed | tf_op | source)
XLA Modules:
  0.0 23.6 jit_solution(198078276658248348)
XLA Ops:
  0.0 0.0 copy-start
  0.0 1.4 %copy-done = bf16[3,128,2048]{2,1,0:T(8,128)(2,1)S(1)} copy-done((bf16[3,128,2048]{2,1,0:T(8,128)(2,1)S(1)}, bf16[3,128,2048]{2,1,0:T(8,128)(2,1)}, u32[]{:S(2)}) %copy-start) | copy-done | bytes 1572888
  1.4 0.0 copy-start.1
  1.4 1.0 %copy-done.1 = f32[3,3,8192]{2,1,0:T(4,128)S(1)} copy-done((f32[3,3,8192]{2,1,0:T(4,128)S(1)}, f32[3,3,8192]{2,1,0:T(4,128)}, u32[]{:S(2)}) %copy-start.1) | copy-done | bytes 294936
  2.4 0.0 copy-start.2
  2.4 0.7 %copy-done.2 = f32[4,512]{1,0:T(4,128)S(1)} copy-done((f32[4,512]{1,0:T(4,128)S(1)}, f32[4,512]{1,0:T(4,128)}, u32[]{:S(2)}) %copy-start.2) | copy-done | bytes 8216
  3.1 0.0 copy-start.3
  3.1 0.7 %copy-done.3 = f32[4,512]{1,0:T(4,128)S(1)} copy-done((f32[4,512]{1,0:T(4,128)S(1)}, f32[4,512]{1,0:T(4,128)}, u32[]{:S(2)}) %copy-start.3) | copy-done | bytes 8216
  3.8 19.0 %shard_map.46 = bf16[128,2048]{1,0:T(8,128)(2,1)S(1)} custom-call(bf16[3,128,2048]{2,1,0:T(8,128)(2,1)S(1)} %copy-done, f32[3,3,8192]{2,1,0:T(4,128)S(1)} %copy-done.1, f32[4,512]{1,0:T(4,128)S(1)} %copy-done.2, f32[4,512]{1,0:T(4,128)S(1)} %copy-done.3), custom_call_target="tpu_custom_call" | custom-call | flops 33554432 | bytes 2097152 | tf_op jit(solution)/shard_map/pallas_call | solution.py:363
  22.8 0.8 %copy.6 = bf16[128,2048]{1,0:T(8,128)(2,1)} copy(bf16[128,2048]{1,0:T(8,128)(2,1)S(1)} %shard_map.46) | data formatting | bytes 1048576
Async XLA Ops:
  0.0 1.4 %copy-start = (bf16[3,128,2048]{2,1,0:T(8,128)(2,1)S(1)}, bf16[3,128,2048]{2,1,0:T(8,128)(2,1)}, u32[]{:S(2)}) copy-start(bf16[3,128,2048]{2,1,0:T(8,128)(2,1)} %stream.1) | copy-start | bytes 4718596
  1.4 1.0 %copy-start.1 = (f32[3,3,8192]{2,1,0:T(4,128)S(1)}, f32[3,3,8192]{2,1,0:T(4,128)}, u32[]{:S(2)}) copy-start(f32[3,3,8192]{2,1,0:T(4,128)} %taps.1) | copy-start | bytes 884740
  2.4 0.7 %copy-start.2 = (f32[4,512]{1,0:T(4,128)S(1)}, f32[4,512]{1,0:T(4,128)}, u32[]{:S(2)}) copy-start(f32[4,512]{1,0:T(4,128)} %rate.1) | copy-start | bytes 24580
  3.1 0.7 %copy-start.3 = (f32[4,512]{1,0:T(4,128)S(1)}, f32[4,512]{1,0:T(4,128)}, u32[]{:S(2)}) copy-start(f32[4,512]{1,0:T(4,128)} %resid.1) | copy-start | bytes 24580

commit v2 on v1

--- a/solution.py
+++ b/solution.py
@@ -9,7 +9,8 @@
 
 GROUP = 16
 LANES = 128
-CHUNKS = 2
+CHUNKS = 4
+PARTS = 2
 DICT = pl.DeviceIdType.MESH
 
 
@@ -82,8 +83,8 @@
             src_ref=src, dst_ref=dst.at[owner], send_sem=dp_send.at[which, d - 1],
             recv_sem=dp_recv.at[which, d - 1], device_id={"dp": peer}, device_id_type=DICT)
 
-    for d in range(1, n_dp):
-        for which in range(2):
+    for which in range(2):
+        for d in range(1, n_dp):
             dp_copy(which, d, dp, lax.rem(dp + d, n_dp)).start()
 
     for c in loads:
@@ -126,33 +127,41 @@
             put(prod, b, j, feature(1, j, window_at(1, j, b)) * feature(2, j, window_at(2, j, b)))
 
     own_rate.wait()
-    own_resid.wait()
     for d in range(1, n_dp):
-        for which in range(2):
-            dp_copy(which, d, lax.rem(dp + n_dp - d, n_dp), dp).wait_recv()
+        dp_copy(0, d, lax.rem(dp + n_dp - d, n_dp), dp).wait_recv()
 
     per_tile = LANES // GROUP
-    tile_of = lax.broadcasted_iota(jnp.int32, (HJ, G), 1) // per_tile
-    row = lax.broadcasted_iota(jnp.int32, (HJ, G), 0)
+    groups = C // GROUP
+    width = sel.shape[1]
+    base = dp * groups
+    window_start = base // width * width
+    tile_of = (lax.broadcasted_iota(jnp.int32, (HJ, width), 1) - (base - window_start)) // per_tile
+    row = lax.broadcasted_iota(jnp.int32, (HJ, width), 0)
     spread = (
-        lax.rem(lax.broadcasted_iota(jnp.int32, (G, LANES), 0), per_tile)
-        == lax.broadcasted_iota(jnp.int32, (G, LANES), 1) // GROUP
+        lax.rem(lax.broadcasted_iota(jnp.int32, (width, LANES), 0), per_tile)
+        == lax.broadcasted_iota(jnp.int32, (width, LANES), 1) // GROUP
     ).astype(f32)
-    for source, is_rate in ((rates, True), (resids, False)):
+    shown = pl.ds(pl.multiple_of(window_start, LANES), width)
+
+    def widen(source, use):
         for h in range(2):
-            mask = tile_of == dp * J + h * HJ + row
+            mask = tile_of == h * HJ + row
             for r in range(R):
-                line = source[r // own_poles, r % own_poles:r % own_poles + 1, :]
+                line = source[r // own_poles, r % own_poles:r % own_poles + 1, shown]
                 sel[(h * R + r) * HJ:(h * R + r + 1) * HJ, :] = jnp.where(mask, line, 0.0)
         wide = jnp.dot(sel[...], spread, precision=lax.Precision.HIGHEST, preferred_element_type=f32)
         for h in range(2):
             for r in range(R):
-                part = wide[(h * R + r) * HJ:(h * R + r + 1) * HJ]
-                if is_rate:
-                    dec[h, r] = jnp.exp(-part)
-                    span[h, r] = jnp.exp(-part * T)
-                else:
-                    amp[h, r] = part
+                use(h, r, wide[(h * R + r) * HJ:(h * R + r + 1) * HJ])
+
+    def use_rate(h, r, part):
+        dec[h, r] = jnp.exp(-part)
+        span[h, r] = jnp.exp(-part * T)
+
+    def use_resid(h, r, part):
+        amp[h, r] = part
+
+    widen(rates, use_rate)
 
     @pl.when(k == 0)
     def _():
@@ -171,35 +180,40 @@
     def rows(tb, h, u):
         return pl.ds(tb * (J * 8) + h * (HJ * 8) + u, HJ, stride=8)
 
-    def close(h):
-        decay = [dec[h, r] for r in range(R)]
+    RP = R // PARTS
+
+    def close(part):
+        slots = [(h, r) for h in range(2) for r in range(part * RP, (part + 1) * RP)]
+        decay = [dec[h, r] for h, r in slots]
 
         def body(tb, state):
             for u in range(8):
-                x = prod[rows(tb, h, u), :]
-                state = tuple(a * s + x for a, s in zip(decay, state))
+                x = [prod[rows(tb, h, u), :] for h in range(2)]
+                state = tuple(a * s + x[slot[0]] for slot, a, s in zip(slots, decay, state))
             return state
 
-        state = lax.fori_loop(0, T // 8, body, tuple(jnp.zeros((HJ, LANES), f32) for _ in range(R)))
-        for r in range(R):
-            end[h, r] = state[r]
-
-    def end_copy(h):
+        state = lax.fori_loop(0, T // 8, body, tuple(jnp.zeros((HJ, LANES), f32) for _ in slots))
+        for (h, r), value in zip(slots, state):
+            end[h, r] = value
+
+    def end_copy(h, part):
+        piece = pl.ds(part * RP, RP)
         return pltpu.make_async_remote_copy(
-            src_ref=end.at[h], dst_ref=end_in.at[h], send_sem=end_send.at[h], recv_sem=end_recv.at[h],
-            device_id={"ctx": partner}, device_id_type=DICT)
-
-    close(1 - core)
-    end_copy(1 - core).start()
-    close(core)
+            src_ref=end.at[h, piece], dst_ref=end_in.at[h, piece], send_sem=end_send.at[h, part],
+            recv_sem=end_recv.at[h, part], device_id={"ctx": partner}, device_id_type=DICT)
+
+    for part in range(PARTS):
+        close(part)
+        end_copy(1 - core, part).start()
 
     @pl.when(core == 0)
     def _():
-        end_copy(0).start()
-
-    def total_of_chip():
-        end_copy(core).wait_recv()
-        for r in range(R):
+        for part in range(PARTS):
+            end_copy(0, part).start()
+
+    def total_of_chip(part):
+        end_copy(core, part).wait_recv()
+        for r in range(part * RP, (part + 1) * RP):
             own, other = end[core, r], end_in[core, r]
             first = jnp.where(core == 0, own, other)
             second = jnp.where(core == 0, other, own)
@@ -228,16 +242,23 @@
 
             forward(c).start()
 
-    total_of_chip()
+    for part in range(PARTS):
+        total_of_chip(part)
+
+        @pl.when(jnp.logical_and(z == 0, has_next))
+        def _():
+            for c in range(part * RP // RC, (part + 1) * RP // RC):
+                chain_copy(c).start()
 
     @pl.when(z == 0)
     def _():
-        for c in range(CHUNKS):
-            @pl.when(has_next)
-            def _():
-                chain_copy(c).start()
         chain_in[...] = jnp.zeros_like(chain_in)
         other_in[...] = jnp.zeros_like(other_in)
+
+    own_resid.wait()
+    for d in range(1, n_dp):
+        dp_copy(1, d, lax.rem(dp + n_dp - d, n_dp), dp).wait_recv()
+    widen(resids, use_resid)
 
     for j in range(J):
         put(query, 0, j, feature(0, j, window_first(0, j)))
@@ -263,21 +284,26 @@
 
         lax.fori_loop(0, T // 8, body, tuple(jnp.zeros((HJ, LANES), f32) for _ in range(R)))
 
+    @pl.when(z == 1)
+    def _():
+        relay()
+
     inside(0)
 
-    @pl.when(z == 1)
+    @pl.when(z == 2)
     def _():
         relay()
 
     inside(1)
 
-    @pl.when(z > 1)
+    @pl.when(z > 2)
     def _():
         relay()
 
     @pl.when(core == 1)
     def _():
-        end_copy(0).wait_recv()
+        for part in range(PARTS):
+            end_copy(0, part).wait_recv()
 
     def tail(h, source):
         for r in range(R):
@@ -301,7 +327,19 @@
 
         lax.fori_loop(0, T // 8, body, tuple(amp[h, r] * zs[r] for r in range(R)))
 
+    def gate(h):
+        @pl.loop(0, blocks)
+        def _(b):
+            for j in range(HJ):
+                tiles = []
+                for u in range(2):
+                    at = pl.ds(pl.multiple_of(((2 * b + u) * J + h * HJ + j) * 8, 8), 8)
+                    tiles.append(query[at, :] * conv[at, :])
+                cols = pl.ds(pl.multiple_of((h * HJ + j) * LANES, LANES), LANES)
+                out[pl.ds(pl.multiple_of(b * 16, 16), 16), cols] = jnp.concatenate(tiles, 0).astype(out.dtype)
+
     tail(core, chain_in)
+    gate(core)
 
     @pl.when(has_prev)
     def _():
@@ -309,16 +347,7 @@
             forward(c).wait_recv()
 
     tail(1 - core, other_in)
-
-    @pl.loop(0, blocks)
-    def _(b):
-        for j in range(J):
-            tiles = []
-            for u in range(2):
-                at = pl.ds(pl.multiple_of(((2 * b + u) * J + j) * 8, 8), 8)
-                tiles.append(query[at, :] * conv[at, :])
-            out[pl.ds(pl.multiple_of(b * 16, 16), 16), pl.ds(j * LANES, LANES)] = jnp.concatenate(
-                tiles, 0).astype(out.dtype)
+    gate(1 - core)
 
     for d in range(1, n_dp):
         for which in range(2):
@@ -328,11 +357,13 @@
     def _():
         halo().wait_send()
 
-    end_copy(1 - core).wait_send()
+    for part in range(PARTS):
+        end_copy(1 - core, part).wait_send()
 
     @pl.when(core == 0)
     def _():
-        end_copy(0).wait_send()
+        for part in range(PARTS):
+            end_copy(0, part).wait_send()
 
     for c in range(CHUNKS):
         @pl.when(has_next)
@@ -373,19 +404,19 @@
                 edge, edge,
                 pltpu.VMEM((3, 24, C), f32),
                 flat, flat, flat,
-                pltpu.VMEM((2 * R * HJ, G), f32),
+                pltpu.VMEM((2 * R * HJ, max(C // GROUP, LANES)), f32),
                 halves, halves, halves, halves, halves,
                 piece, piece, piece,
                 pltpu.VMEM((R, HJ, LANES), f32),
                 dma((6,)),
                 dma((2, n_dp - 1)), dma((2, n_dp - 1)),
                 dma((2,)),
-                dma((2,)), dma((2,)),
+                dma((2, PARTS)), dma((2, PARTS)),
                 dma((CHUNKS,)), dma((CHUNKS,)),
                 dma((CHUNKS,)), dma((CHUNKS,)),
             ],
             compiler_params=pltpu.CompilerParams(
-                collective_id=0, has_side_effects=True, vmem_limit_bytes=32 * 1024 * 1024),
+                collective_id=0, has_side_effects=True, vmem_limit_bytes=60 * 1024 * 1024),
             cost_estimate=pl.CostEstimate(
                 flops=8 * R * T * C, bytes_accessed=8 * T * C, transcendentals=0),
         )(stream, short_taps, decay_rate, residue)

time: 23.9 us -> 20.7 us (0.87)
  local copies, waits for them, and re-layouts: 4.59 us -> 1.88 us
  Pallas kernels: 19 us -> 18.7 us
    unnamed x9 -> x1, local copies, waits for them, and re-layouts: 4.59 us -> 1.88 us
    pallas_call x1, Pallas kernels: 19 us -> 18.7 us  [shards(): pl.pallas_call(functools.partial(kernel, n_ctx, n_dp), out_shape=jax.Shap...]
where the time goes in v2:
time: 20.7 us; the launch traced here: 20.6 us
  Pallas kernels  18.7 us (90%)
  local copies, waits for them, and re-layouts  1.88 us (9%)
    pallas_call x1, Pallas kernels, shards(): pl.pallas_call(functools.partial(kernel, n_ctx, n_dp), out_shape=jax.Shap...  18.7 us
    unnamed x1, local copies, waits for them, and re-layouts  1.88 us

profile of v2, /device:TPU:25, one launch (start us, length us, event | category | flops | bytes accessed | tf_op | source)
XLA Modules:
  0.0 20.6 jit_solution(95177813584583627)
XLA Ops:
  0.0 18.7 %shard_map.46 = bf16[128,2048]{1,0:T(8,128)(2,1)} custom-call(bf16[3,128,2048]{2,1,0:T(8,128)(2,1)} %stream.1, f32[3,3,8192]{2,1,0:T(4,128)} %taps.1, f32[4,512]{1,0:T(4,128)} %rate.1, f32[4,512]{1,0:T(4,128)} %resid.1), custom_call_target="tpu_custom_call" | custom-call | flops 33554432 | bytes 2097152 | tf_op jit(solution)/shard_map/pallas_call | solution.py:394
  18.7 1.9 %copy.6 = bf16[128,2048]{1,0:T(8,128)(2,1)} copy(bf16[128,2048]{1,0:T(8,128)(2,1)} %shard_map.46) | data formatting | bytes 1048576

commit v3 on v2

--- a/solution.py
+++ b/solution.py
@@ -393,7 +393,7 @@
         edge = pltpu.VMEM((3, n_taps - 1, C), f32)
         return pl.pallas_call(
             functools.partial(kernel, n_ctx, n_dp),
-            out_shape=jax.ShapeDtypeStruct((T, C), jnp.bfloat16),
+            out_shape=pltpu.VMEM((T, C), jnp.bfloat16),
             in_specs=[pl.BlockSpec(memory_space=pl.ANY)] * 4,
             out_specs=pl.BlockSpec(memory_space=pltpu.VMEM),
             scratch_shapes=[
@@ -416,7 +416,7 @@
                 dma((CHUNKS,)), dma((CHUNKS,)),
             ],
             compiler_params=pltpu.CompilerParams(
-                collective_id=0, has_side_effects=True, vmem_limit_bytes=60 * 1024 * 1024),
+                collective_id=0, has_side_effects=True, vmem_limit_bytes=56 * 1024 * 1024),
             cost_estimate=pl.CostEstimate(
                 flops=8 * R * T * C, bytes_accessed=8 * T * C, transcendentals=0),
         )(stream, short_taps, decay_rate, residue)

time: 20.7 us -> 18.8 us (0.908)
  local copies, waits for them, and re-layouts: 1.88 us -> 0.8 us
  Pallas kernels: 18.7 us -> 17.9 us
    unnamed x1, local copies, waits for them, and re-layouts: 1.88 us -> 0.8 us
    pallas_call x1, Pallas kernels: 18.7 us -> 17.9 us  [shards(): pl.pallas_call(functools.partial(kernel, n_ctx, n_dp), out_shape=pltpu.VM...]
where the time goes in v3:
time: 18.8 us; the launch traced here: 18.7 us
  Pallas kernels  17.9 us (95%)
  local copies, waits for them, and re-layouts  0.8 us (4%)
    pallas_call x1, Pallas kernels, shards(): pl.pallas_call(functools.partial(kernel, n_ctx, n_dp), out_shape=pltpu.VM...  17.9 us
    unnamed x1, local copies, waits for them, and re-layouts  0.8 us

profile of v3, /device:TPU:25, one launch (start us, length us, event | category | flops | bytes accessed | tf_op | source)
XLA Modules:
  0.0 18.7 jit_solution(7638921210969149620)
XLA Ops:
  0.0 17.9 %shard_map.46 = bf16[128,2048]{1,0:T(8,128)(2,1)S(1)} custom-call(bf16[3,128,2048]{2,1,0:T(8,128)(2,1)} %stream.1, f32[3,3,8192]{2,1,0:T(4,128)} %taps.1, f32[4,512]{1,0:T(4,128)} %rate.1, f32[4,512]{1,0:T(4,128)} %resid.1), custom_call_target="tpu_custom_call" | custom-call | flops 33554432 | bytes 2097152 | tf_op jit(solution)/shard_map/pallas_call | solution.py:394
  17.9 0.8 %copy.6 = bf16[128,2048]{1,0:T(8,128)(2,1)} copy(bf16[128,2048]{1,0:T(8,128)(2,1)S(1)} %shard_map.46) | data formatting | bytes 1048576

commit v4 on v3

--- a/solution.py
+++ b/solution.py
@@ -78,11 +78,13 @@
     )
 
     def dp_copy(which, d, owner, peer):
-        src, dst = ((rate, rates), (resid, resids))[which]
+        dst = (rates, resids)[which]
         return pltpu.make_async_remote_copy(
-            src_ref=src, dst_ref=dst.at[owner], send_sem=dp_send.at[which, d - 1],
+            src_ref=dst.at[dp], dst_ref=dst.at[owner], send_sem=dp_send.at[which, d - 1],
             recv_sem=dp_recv.at[which, d - 1], device_id={"dp": peer}, device_id_type=DICT)
 
+    own_rate.wait()
+    own_resid.wait()
     for which in range(2):
         for d in range(1, n_dp):
             dp_copy(which, d, dp, lax.rem(dp + d, n_dp)).start()
@@ -126,7 +128,6 @@
         for j in range(J):
             put(prod, b, j, feature(1, j, window_at(1, j, b)) * feature(2, j, window_at(2, j, b)))
 
-    own_rate.wait()
     for d in range(1, n_dp):
         dp_copy(0, d, lax.rem(dp + n_dp - d, n_dp), dp).wait_recv()
 
@@ -255,7 +256,6 @@
         chain_in[...] = jnp.zeros_like(chain_in)
         other_in[...] = jnp.zeros_like(other_in)
 
-    own_resid.wait()
     for d in range(1, n_dp):
         dp_copy(1, d, lax.rem(dp + n_dp - d, n_dp), dp).wait_recv()
     widen(resids, use_resid)

time: 18.8 us -> 18.6 us (0.989)
  Pallas kernels: 17.9 us -> 17.7 us
    pallas_call x1, Pallas kernels: 17.9 us -> 17.7 us  [shards(): pl.pallas_call(functools.partial(kernel, n_ctx, n_dp), out_shape=pltpu.VM...]
where the time goes in v4:
time: 18.6 us; the launch traced here: 18.5 us
  Pallas kernels  17.7 us (95%)
  local copies, waits for them, and re-layouts  0.8 us (4%)
    pallas_call x1, Pallas kernels, shards(): pl.pallas_call(functools.partial(kernel, n_ctx, n_dp), out_shape=pltpu.VM...  17.7 us
    unnamed x1, local copies, waits for them, and re-layouts  0.8 us

profile of v4, /device:TPU:25, one launch (start us, length us, event | category | flops | bytes accessed | tf_op | source)
XLA Modules:
  0.0 18.5 jit_solution(921662419575592902)
XLA Ops:
  0.0 17.7 %shard_map.46 = bf16[128,2048]{1,0:T(8,128)(2,1)S(1)} custom-call(bf16[3,128,2048]{2,1,0:T(8,128)(2,1)} %stream.1, f32[3,3,8192]{2,1,0:T(4,128)} %taps.1, f32[4,512]{1,0:T(4,128)} %rate.1, f32[4,512]{1,0:T(4,128)} %resid.1), custom_call_target="tpu_custom_call" | custom-call | flops 33554432 | bytes 2097152 | tf_op jit(solution)/shard_map/pallas_call | solution.py:394
  17.7 0.8 %copy.6 = bf16[128,2048]{1,0:T(8,128)(2,1)} copy(bf16[128,2048]{1,0:T(8,128)(2,1)S(1)} %shard_map.46) | data formatting | bytes 1048576
